TPU v7x, 768 devices: a whole 4x8x12 slice. The times are simulated.
768 devices in a mesh: tok: 64 (over z_lo, y, core), fin: 4 (over x), fout: 3 (over z_hi).
Axes of the slice: x: 4, y: 8, z: 12 (z_hi: 3, z_lo: 4; z = z_hi * 4 + z_lo), core: 2. Of those that a mesh axis runs over, the one named last changes fastest.
Arguments:
- tokens: bfloat16 [384, 6144], P('tok', 'fin'), may hold values from -6 to 6
- cotangent: bfloat16 [384, 6144], P('tok', 'fin'), may hold values from -6 to 6
- image_lengths: int32 [16], replicated, may hold values from 1 to 48, 336 in all
- fc1_weight: bfloat16 [6144, 24576], P('fin', ('tok', 'fout')), may hold values from -0.078125 to 0.078125
- fc2_weight: bfloat16 [24576, 6144], P(('tok', 'fout'), 'fin'), may hold values from -0.0390625 to 0.0390625
Outputs:
- block_out: bfloat16 [384, 6144], P('tok', 'fin')
- grad_tokens: bfloat16 [384, 6144], P('tok', 'fin')
- grad_fc1: float32 [6144, 24576], P('fin', ('tok', 'fout'))
- grad_fc2: float32 [24576, 6144], P(('tok', 'fout'), 'fin')
Inputs may be any that keep to these rules, and one draw needn't show every extreme that they name: `image_lengths`: the spans together cover 7 * 48 rows; the rest are padding rows. Some image has exactly 48 patches.
All inputs are finite; a program needn't handle non-finite values.
Results may differ from a plain program's by a relative error of at most 0.012.
Values may be sent and summed in bfloat16 or wider, within the bound.
A program may use at most 32 MiB of HBM per device.

v0:
```python
import jax
import jax.numpy as jnp
from jax import lax
from jax.sharding import PartitionSpec as P

inv_root_two = 0.7071067811865476
inv_root_two_pi = 0.3989422804014327


def row_weights(lengths, first_row, row_count, longest):
    span_ends = jnp.cumsum(lengths, dtype=jnp.int32)
    starts = span_ends - lengths
    position = first_row + jnp.arange(row_count, dtype=jnp.int32)
    inside = (position[:, None] >= starts[None, :]) & (position[:, None] < span_ends[None, :])
    span_len = jnp.sum(jnp.where(inside, lengths[None, :], 0), axis=1)
    is_valid = jnp.any(inside, axis=1)
    length_ratio = jnp.float32(longest) / jnp.maximum(span_len, 1).astype(jnp.float32)
    return jnp.where(is_valid, jnp.sqrt(length_ratio), jnp.float32(0.0))


def activations(preact, grad_act):
    normal_cdf = 0.5 * (1.0 + lax.erf(preact * inv_root_two))
    density = jnp.exp(-0.5 * preact * preact) * inv_root_two_pi
    activated = (preact * normal_cdf).astype(jnp.bfloat16)
    grad_pre = (grad_act * (normal_cdf + preact * density)).astype(jnp.bfloat16)
    return (activated, grad_pre)


def per_device(tokens, cotangent, image_lengths, fc1_weight, fc2_weight):
    tok_rows = tokens.shape[0]
    feat_width = tokens.shape[1]
    total_rows = tok_rows * lax.axis_size("tok")
    first_row = lax.axis_index("tok") * tok_rows
    scaling = row_weights(image_lengths, first_row, tok_rows, total_rows // 8)
    scaled = (cotangent.astype(jnp.float32) * scaling[:, None]).astype(jnp.bfloat16)
    all_tokens, all_scaled = (
        lax.all_gather(tokens, "tok", axis=0, tiled=True),
        lax.all_gather(scaled, "tok", axis=0, tiled=True),
    )
    pre_part = jnp.dot(all_tokens, fc1_weight, preferred_element_type=jnp.float32)
    back_part = lax.dot_general(
        all_scaled, fc2_weight, (((1,), (1,)), ((), ())), preferred_element_type=jnp.float32
    )
    pre_share, back_share = (
        lax.psum_scatter(pre_part, "fin", scatter_dimension=0, tiled=True),
        lax.psum_scatter(back_part, "fin", scatter_dimension=0, tiled=True),
    )
    act_share, grad_share = activations(pre_share, back_share)
    activated, grad_pre = (
        lax.all_gather(act_share, "fin", axis=0, tiled=True),
        lax.all_gather(grad_share, "fin", axis=0, tiled=True),
    )
    grad_fc2 = lax.dot_general(
        activated, all_scaled, (((0,), (0,)), ((), ())), preferred_element_type=jnp.float32
    )
    grad_fc1 = lax.dot_general(
        all_tokens, grad_pre, (((0,), (0,)), ((), ())), preferred_element_type=jnp.float32
    )
    forward = jnp.dot(activated, fc2_weight, preferred_element_type=jnp.float32)
    backward = lax.dot_general(
        grad_pre, fc1_weight, (((1,), (1,)), ((), ())), preferred_element_type=jnp.float32
    )
    row_share = lax.psum_scatter(
        jnp.concatenate([forward, backward], axis=1),
        ("tok", "fout"),
        scatter_dimension=0,
        tiled=True,
    )
    rounded = lax.all_gather(row_share.astype(jnp.bfloat16), "fout", axis=0, tiled=True)
    block_out = rounded[:, :feat_width]
    grad_tokens = rounded[:, feat_width:]
    return (block_out, grad_tokens, grad_fc1, grad_fc2)


def solution(mesh):
    return jax.shard_map(
        per_device,
        mesh=mesh,
        in_specs=(
            P("tok", "fin"),
            P("tok", "fin"),
            P(),
            P("fin", ("tok", "fout")),
            P(("tok", "fout"), "fin"),
        ),
        out_specs=(
            P("tok", "fin"),
            P("tok", "fin"),
            P("fin", ("tok", "fout")),
            P(("tok", "fout"), "fin"),
        ),
        check_vma=False,
    )
```

profile of v0, /device:TPU:192, one launch (start us, length us, event | category | flops | bytes accessed | tf_op | source)
XLA Modules:
  0.0 1545.1 jit_solution(16472626095810540786)
XLA Ops:
  7.2 0.0 copy-start
  7.2 0.0 copy-start.2
  7.2 0.0 all-gather.8.cloned.1.call-start
  7.3 0.8 copy.15
  8.1 0.1 reduce
  8.2 0.7 sub.3
  8.9 0.8 select_reduce_fusion
  9.7 0.2 fusion.8
  9.9 1.4 fusion.6
  11.4 0.0 all-gather.8.cloned.1.call-update
  11.4 0.0 all-gather.6.cloned.1.call-start
  11.4 0.7 all-gather.6.cloned.1.call-update
  12.1 0.0 reduce-scatter.5.cloned.1.call-start
  12.2 122.7 %all-gather.8.cloned.1.call-done = bf16[64,6,1536]{2,1,0:T(8,128)(2,1)} async-done(((bf16[1,6,1536]{2,1,0:T(8,128)(2,1)}), bf16[64,6,1536]{2,1,0:T(8,128)(2,1)}) %all-gather.8.cloned.1.call-update) | async-done | bytes 1179664 | tf_op jit(solution)/shard_map/all_gather | solution.py:38
  134.9 2.3 reshape.51
  137.2 0.0 copy-done.2
  137.2 1.1 fusion.12
  138.3 0.0 reduce-scatter.5.cloned.1.call-update
  138.4 0.0 reduce-scatter.3.cloned.1.call-start
  138.4 117.4 %all-gather.6.cloned.1.call-done = bf16[64,6,1536]{2,1,0:T(8,128)(2,1)} async-done(((bf16[1,6,1536]{2,1,0:T(8,128)(2,1)}), bf16[64,6,1536]{2,1,0:T(8,128)(2,1)}) %all-gather.6.cloned.1.call-update) | async-done | bytes 1179664 | tf_op jit(solution)/shard_map/all_gather | solution.py:37
  255.8 2.3 reshape.49
  258.1 0.0 copy-done
  258.1 1.1 fusion.10
  259.3 0.0 reduce-scatter.3.cloned.1.call-update
  259.3 1.3 dynamic-slice
  261.2 26.5 %reduce-scatter.5.cloned.1.call-done = f32[96,128]{1,0:T(8,128)} async-done(((f32[384,128]{1,0:T(8,128)}), f32[96,128]{1,0:T(8,128)}) %reduce-scatter.5.cloned.1.call-update) | async-done | bytes 49168 | tf_op jit(solution)/shard_map/reduce_scatter | solution.py:46
  287.8 32.3 %reduce-scatter.3.cloned.1.call-done = f32[96,128]{1,0:T(8,128)} async-done(((f32[384,128]{1,0:T(8,128)}), f32[96,128]{1,0:T(8,128)}) %reduce-scatter.3.cloned.1.call-update) | async-done | bytes 49168 | tf_op jit(solution)/shard_map/reduce_scatter | solution.py:45
  320.0 0.9 multiply_convert_fusion.1
  320.9 11.9 all_gather.18
  332.8 0.4 convolution_bitcast_fusion
  333.2 1.9 fusion.13
  335.1 0.0 copy-start.3
  335.1 12.0 all_gather.16
  347.1 1.3 fusion.14
  348.4 0.0 copy-done.3
  348.4 0.0 copy-start.1
  348.4 1.9 fusion.11
  350.3 1.1 copy.16
  351.5 0.0 copy-done.1
  351.5 4.2 pad_maximum_fusion
  355.7 1169.5 %all-reduce.2 = bf16[384,3072]{1,0:T(8,128)(2,1)S(1)} all-reduce(f32[384,3072]{1,0:T(8,128)} %pad_maximum_fusion), channel_id=4, replica_groups=mesh['tok'=64,'fin'=4,'fout'=3] {'tok','fout'}, use_global_device_ids=true, to_apply=%region_5.6.clone | all-reduce | flops 1179648 | bytes 7077888
  1525.2 12.8 all-gather.2
  1538.0 0.6 fusion.9
  (5 shorter events, 0.1 us)
Async XLA Ops:
  7.2 250.9 %copy-start = (bf16[1536,128]{1,0:T(8,128)(2,1)S(1)}, bf16[1536,128]{1,0:T(8,128)(2,1)}, u32[]{:S(2)}) copy-start(bf16[1536,128]{1,0:T(8,128)(2,1)} %param.8) | copy-start | bytes 1179652
  7.2 130.0 %copy-start.2 = (bf16[128,1536]{1,0:T(8,128)(2,1)S(1)}, bf16[128,1536]{1,0:T(8,128)(2,1)}, u32[]{:S(2)}) copy-start(bf16[128,1536]{1,0:T(8,128)(2,1)} %param.9) | copy-start | bytes 1179652
  7.2 127.7 %all-gather.8.cloned.1.call-start = ((), (), s32[]{:S(2)}) async-start(), calls=%async_computation.5 | async-start | bytes 1597440 | tf_op jit(solution)/shard_map/all_gather | solution.py:38
  11.4 244.4 %all-gather.6.cloned.1.call-start = ((), (), s32[]{:S(2)}) async-start(), calls=%async_computation.4 | async-start | bytes 1597440 | tf_op jit(solution)/shard_map/all_gather | solution.py:37
  12.1 275.6 %reduce-scatter.5.cloned.1.call-start = ((), (), s32[]{:S(2)}) async-start(), calls=%async_computation.3 | async-start | bytes 245760 | tf_op jit(solution)/shard_map/reduce_scatter | solution.py:46
  138.4 181.6 %reduce-scatter.3.cloned.1.call-start = ((), (), s32[]{:S(2)}) async-start(), calls=%async_computation.2 | async-start | bytes 245760 | tf_op jit(solution)/shard_map/reduce_scatter | solution.py:45
  335.1 13.3 copy-start.3
  348.4 3.0 copy-start.1
Sparse Core Ops, SparseCore 0:
  11.5 123.3 all-gather.7
  137.3 118.4 all-gather.5
  259.5 28.2 reduce-scatter.4
  291.6 28.3 reduce-scatter.2
where the time goes:
time: 1550 us
  blocking collectives  1210 us (78%)
  waiting for transfers between devices  300 us (19%)
    unnamed x1, blocking collectives  1170 us
    all_gather x1, waiting for transfers between devices, per_device(): lax.all_gather(scaled, 'tok', axis=0, tiled=True)  123 us
    all_gather x1, waiting for transfers between devices, per_device(): lax.all_gather(tokens, 'tok', axis=0, tiled=True)  117 us
    reduce_scatter x1, waiting for transfers between devices, per_device(): lax.psum_scatter(pre_part, 'fin', scatter_dimension=0, tiled=True)  32.3 us
  transfers between devices with their start and end apart: 4, of which 4 were waited for; matrix products, arithmetic and copies ran while one was open for 1% of the time, Pallas kernels for 0%

commit v1 on v0

v1 whole, which is shorter than its diff:
```python
import jax
import jax.numpy as jnp
from jax import lax
from jax.experimental import pallas as pl
from jax.experimental.pallas import tpu as pltpu
from jax.sharding import PartitionSpec as P

inv_root_two = 0.7071067811865476
inv_root_two_pi = 0.3989422804014327

NX, NY, NL, NH = 4, 8, 4, 3
NZ = NL * NH
ROWS = 6
BLOCK = 16
FEAT = 1536
HID = 128
LONGEST = 48
CA, CB = 256, 512
A0, A1 = 0, 2 * CA
N_SEMS = 80

bf16, f32 = jnp.bfloat16, jnp.float32


def kernel(
    tok_ref, cot_ref, len_ref, w1_ref, w2_ref,
    out_ref, gtok_ref, g1_ref, g2_ref,
    xb, xa, xbb, xsa, xsb, wc, wt,
    rs, rr, rown, ag, ags,
    ya, yb, ras, rar, rzs, rz, rz2,
    rbs, rbr, rys, ry, vha, vhb,
    mt, g1v, g2v,
    send_sem, recv_sem, local_sem,
):
    t = lax.axis_index("tok")
    x = lax.axis_index("fin")
    f = lax.axis_index("fout")
    c = lax.rem(t, 2)
    y = lax.rem(lax.div(t, 2), NY)
    zl = lax.div(t, 2 * NY)
    z = f * NL + zl

    def on_y(d):
        return {"tok": (zl * NY + lax.rem(y + d + NY, NY)) * 2 + c}

    def on_z(d):
        far = lax.rem(z + d + NZ, NZ)
        return {
            "tok": (lax.rem(far, NL) * NY + y) * 2 + c,
            "fout": lax.div(far, NL),
        }

    def on_x(d):
        return {"fin": lax.rem(x + d, NX)}

    sibling = {"tok": t + 1 - 2 * c}

    def cls(d):
        return lax.rem(zl + d + NL, NL)

    def row(d):
        return lax.rem(y + d + NY, NY)

    sent = []

    def send(src, dst, device):
        i = len(sent)
        copy = pltpu.make_async_remote_copy(
            src_ref=src, dst_ref=dst,
            send_sem=send_sem.at[i], recv_sem=recv_sem.at[i],
            device_id=device, device_id_type=pl.DeviceIdType.MESH,
        )
        copy.start()
        sent.append(copy)
        return copy

    own_w1 = pltpu.make_async_copy(w1_ref, wc.at[:, 0:HID], local_sem.at[0])
    own_w2 = pltpu.make_async_copy(w2_ref, wt.at[0, 0:HID], local_sem.at[1])
    own_w1.start()
    own_w2.start()

    barrier = pltpu.get_barrier_semaphore()
    partners = (
        [sibling]
        + [on_x(d) for d in (1, 2, 3)]
        + [on_y(d) for d in (1, 2, 3, 4, 5, 6, 7)]
        + [on_z(d) for d in (1, -1, 2, -2, 4, -4)]
    )
    for device in partners:
        pl.semaphore_signal(
            barrier, inc=1, device_id=device, device_id_type=pl.DeviceIdType.MESH
        )

    position = t * ROWS + lax.broadcasted_iota(jnp.int32, (8, 128), 0)
    span = jnp.zeros((8, 128), jnp.int32)
    start = jnp.int32(0)
    for i in range(16):
        length = len_ref[i]
        end = start + length
        span = jnp.where((position >= start) & (position < end), length, span)
        start = end
    ratio = f32(LONGEST) / jnp.maximum(span, 1).astype(f32)
    scale = jnp.where(span > 0, jnp.sqrt(ratio), f32(0.0))
    scale = jnp.concatenate([scale] * (FEAT // 128), axis=1)[0:ROWS]
    xb[...] = jnp.zeros_like(xb)
    xb[0:ROWS] = tok_ref[...].astype(f32)
    xb[8 : 8 + ROWS] = cot_ref[...].astype(f32) * scale
    for s in range(2):
        xa[s, y, zl] = xb[:, A0 + s * CA : A0 + (s + 1) * CA].astype(bf16)
        xbb[s, y, zl] = xb[:, A1 + s * CB : A1 + (s + 1) * CB].astype(bf16)

    pl.semaphore_wait(barrier, len(partners))

    ga_z = []
    gb_y = []
    own_a, own_b = xa.at[:, y, zl], xbb.at[:, y, zl]
    for d in (4, 3, 5, 2, 6, 1, 7):
        gb_y.append(send(own_b, own_b, on_y(d)))
    for d in (1, -1):
        ga_z.append(send(own_a, own_a, on_z(d)))
    for s, d in ((0, 2), (1, -2)):
        ga_z.append(send(xa.at[s, y, zl], xa.at[s, y, zl], on_z(d)))
    sib_w1 = send(w1_ref, wc.at[:, HID : 2 * HID], sibling)
    sib_w2 = send(w2_ref, wt.at[0, HID : 2 * HID], sibling)

    own_w1.wait()
    own_w2.wait()
    wc[:, 2 * HID : 3 * HID] = wt[0, 0:HID].T
    wt[1, 0:HID] = wc[:, 0:HID].T

    def ring_steps(way, s):
        return 4 if way == s else 3

    def gather_y(k, way, s):
        sign = 1 if way == 0 else -1
        part = xa.at[s, row(-sign * k)]
        return send(part, part, on_y(sign))

    for copy in ga_z:
        copy.wait_recv()
    ga_y = {}
    for s in range(2):
        for way in range(2):
            ga_y[way, s] = gather_y(0, way, s)

    for copy in gb_y:
        copy.wait_recv()
    gb_z = {}
    for s, d in ((0, 1), (1, -1), (1, 1), (0, -1)):
        part = xbb.at[s, :, zl]
        gb_z[d, s] = send(part, part, on_z(d))

    def ga_step(k):
        for s in range(2):
            for way in range(2):
                if k < ring_steps(way, s):
                    ga_y[way, s].wait_recv()
                    ga_y[way, s] = gather_y(k, way, s)

    ga_step(1)
    sib_w1.wait_recv()
    sib_w2.wait_recv()
    wc[:, 3 * HID : 4 * HID] = wt[0, HID : 2 * HID].T
    wt[1, HID : 2 * HID] = wc[:, HID : 2 * HID].T
    ga_step(2)
    gb_last = []
    for s, d in ((0, 1), (1, -1)):
        gb_z[d, s].wait_recv()
        part = xbb.at[s, :, cls(-d)]
        gb_last.append(send(part, part, on_z(d)))
    ga_step(3)
    for s in range(2):
        for way in range(2):
            ga_y[way, s].wait_recv()
    gb_z[1, 1].wait_recv()
    gb_z[-1, 0].wait_recv()
    for copy in gb_last:
        copy.wait_recv()

    def partial(q):
        rows = pl.ds(2 * q, 2)
        lhs = jnp.concatenate(
            [xa[s, rows].reshape(128, CA) for s in range(2)]
            + [xbb[s, rows].reshape(128, CB) for s in range(2)],
            axis=1,
        )
        pre = jnp.dot(lhs, wc[:, 0 : 2 * HID], preferred_element_type=f32)
        back = jnp.dot(lhs, wc[:, 2 * HID : 4 * HID], preferred_element_type=f32)
        pre = pre.reshape(8, 2, 8, 2 * HID)[:, 0].reshape(2, 32, 2 * HID)
        back = back.reshape(8, 2, 8, 2 * HID)[:, 1].reshape(2, 32, 2 * HID)
        return jnp.concatenate([pre, back], axis=2)

    x_in = []
    for j, d in enumerate((2, 1, 3)):
        rs[j] = partial(lax.rem(x + d, NX)).astype(bf16)
        x_in.append(send(rs.at[j], rr.at[j], on_x(d)))
    rown[...] = partial(x)
    xs = [send(xa, xsa, sibling), send(xbb, xsb, sibling)]
    for copy in x_in:
        copy.wait_recv()
    total = rown[...]
    for j in range(3):
        total = total + rr[j].astype(f32)
    pre, back = total[:, :, 0 : 2 * HID], total[:, :, 2 * HID : 4 * HID]
    cdf = 0.5 * (1.0 + lax.erf(pre * inv_root_two))
    density = jnp.exp(-0.5 * pre * pre) * inv_root_two_pi
    act = (pre * cdf).astype(bf16)
    gp = (back * (cdf + pre * density)).astype(bf16)
    mine = pl.ds(2 * x, 2)
    for j in range(2):
        lanes = slice(j * HID, (j + 1) * HID)
        ag[mine, j] = jnp.concatenate([act[:, :, lanes], gp[:, :, lanes]], axis=2)
    x_out = [send(ag.at[mine], ag.at[mine], on_x(d)) for d in (2, 1, 3)]
    for copy in x_out:
        copy.wait_recv()
    ag_sib = send(ag.at[:, 1], ags, sibling)

    own = ag[:, 0].reshape(256, 2 * HID)
    sib = ag[:, 1].reshape(256, 2 * HID)
    act2 = jnp.concatenate([own[:, 0:HID], sib[:, 0:HID]], axis=1)
    gp2 = jnp.concatenate([own[:, HID:], sib[:, HID:]], axis=1)

    def outputs(dst, s, width, first):
        for n in range(width // 256):
            cols = slice(first + n * 256, first + (n + 1) * 256)
            to = slice(n * 256, (n + 1) * 256)
            fwd = jnp.dot(act2, wt[0, :, cols], preferred_element_type=f32)
            dst[s, :, :, 0:8, to] = fwd.reshape(NY, NL, 8, 256)
            bwd = jnp.dot(gp2, wt[1, :, cols], preferred_element_type=f32)
            dst[s, :, :, 8:16, to] = bwd.reshape(NY, NL, 8, 256)

    for s in range(2):
        outputs(yb, s, CB, A1 + s * CB)
    rb = {}
    for w, (s, d) in enumerate(((0, 1), (1, -1))):
        rbs[w] = yb[s, :, cls(2)].astype(bf16)
        rb[0, w] = send(rbs.at[w], rbr.at[w], on_z(d))
    for w, (s, d) in enumerate(((1, 1), (0, -1))):
        rbs[2 + w] = yb[s, :, cls(d)].astype(bf16)
        rb[1, w] = send(rbs.at[2 + w], rbr.at[2 + w], on_z(d))

    for s in range(2):
        outputs(ya, s, CA, A0 + s * CA)
    ra = {}

    def reduce_y(k, way, s):
        sign = 1 if way == 0 else -1
        slot = (way * 2 + s) * 4
        value = ya[s, row(sign * (ring_steps(way, s) - k))]
        if k > 0:
            ra[way, s].wait_recv()
            value = value + rar[slot + k - 1].astype(f32)
        ras[slot + k] = value.astype(bf16)
        ra[way, s] = send(ras.at[slot + k], rar.at[slot + k], on_y(sign))

    def ra_step(k):
        for s in range(2):
            for way in range(2):
                if k < ring_steps(way, s):
                    reduce_y(k, way, s)

    ra_step(0)

    for copy in xs:
        copy.wait_recv()
    ag_sib.wait_recv()

    def spread(v):
        v = v.astype(f32).reshape(32, 8, 2 * HID)
        none = jnp.zeros((32, 8, HID), f32)
        first = jnp.concatenate([v[:, :, HID:], none], axis=2)
        second = jnp.concatenate([none, v[:, :, 0:HID]], axis=2)
        both = jnp.concatenate([first, second], axis=1)
        return both.reshape(512, 2 * HID).astype(bf16)

    mt[:, 0:512] = spread(ag[:, 0]).T
    mt[:, 512:1024] = spread(ags[...]).T

    def weight_grads(src, src_sib, s, width, first):
        for n in range(width // 256):
            lanes = slice(n * 256, (n + 1) * 256)
            lhs = src[s, :, :, :, lanes].reshape(512, 256)
            rhs = src_sib[s, :, :, :, lanes].reshape(512, 256)
            g = jnp.dot(mt[:, 0:512], lhs, preferred_element_type=f32)
            g = g + jnp.dot(mt[:, 512:1024], rhs, preferred_element_type=f32)
            cols = slice(first + n * 256, first + (n + 1) * 256)
            g1v[cols, :] = g[0:HID].T
            g2v[:, cols] = g[HID:]

    for w, (s, d) in enumerate(((0, 1), (1, -1))):
        rb[0, w].wait_recv()
        value = yb[s, :, cls(d)] + rbr[w].astype(f32)
        rbs[4 + w] = value.astype(bf16)
        rb[2, w] = send(rbs.at[4 + w], rbr.at[4 + w], on_z(d))
    ra_step(1)
    weight_grads(xa, xsa, 0, CA, A0)
    weight_grads(xa, xsa, 1, CA, A0 + CA)
    ra_step(2)
    weight_grads(xbb, xsb, 0, CB, A1)
    for w in range(2):
        rb[1, w].wait_recv()
        rb[2, w].wait_recv()
    for s in range(2):
        near = rbr[4 if s == 0 else 5].astype(f32)
        other = rbr[3 if s == 0 else 2].astype(f32)
        value = yb[s, :, zl] + near + other
        yb[s, :, zl] = value
        rys[:, s] = value.astype(bf16)
    by = []
    for d in (4, 3, 5, 2, 6, 1, 7):
        by.append(send(rys.at[row(d)], ry.at[d - 1], on_y(d)))
    ra_step(3)
    weight_grads(xbb, xsb, 1, CB, A1 + CB)
    out_g1 = pltpu.make_async_copy(g1v, g1_ref, local_sem.at[2])
    out_g2 = pltpu.make_async_copy(g2v, g2_ref, local_sem.at[3])
    out_g1.start()
    out_g2.start()

    for s in range(2):
        value = ya[s, y]
        for way in range(2):
            ra[way, s].wait_recv()
            value = value + rar[(way * 2 + s) * 4 + ring_steps(way, s) - 1].astype(f32)
        ya[s, y] = value
        rzs[s] = value.astype(bf16)
    az = []
    for w, (s, d) in enumerate(((0, 2), (1, -2))):
        az.append(send(rzs.at[s, cls(2)], rz2.at[w], on_z(d)))
    for w, d in enumerate((1, -1)):
        az.append(send(rzs.at[:, cls(d)], rz.at[w], on_z(d)))

    for copy in by:
        copy.wait_recv()
    value = yb[:, y, zl]
    for j in range(NY - 1):
        value = value + ry[j].astype(f32)
    vhb[f] = value.astype(bf16)
    last_b = [send(vhb.at[f], vhb.at[f], on_z(d)) for d in (4, -4)]
    for copy in az:
        copy.wait_recv()
    value = ya[:, y, zl] + rz[0].astype(f32) + rz[1].astype(f32)
    value = value + rz2[...].astype(f32)
    vha[f] = value.astype(bf16)
    last_a = [send(vha.at[f], vha.at[f], on_z(d)) for d in (4, -4)]

    def finish(copies, parts, width, first):
        for copy in copies:
            copy.wait_recv()
        value = parts[0].astype(f32) + parts[1].astype(f32) + parts[2].astype(f32)
        for s in range(2):
            cols = slice(first + s * width, first + (s + 1) * width)
            out_ref[:, cols] = value[s, 0:ROWS].astype(bf16)
            gtok_ref[:, cols] = value[s, 8 : 8 + ROWS].astype(bf16)

    finish(last_b, vhb, CB, A1)
    finish(last_a, vha, CA, A0)

    out_g1.wait()
    out_g2.wait()
    for copy in sent:
        copy.wait_send()


def per_device(tokens, cotangent, image_lengths, fc1_weight, fc2_weight):
    vmem = pl.BlockSpec(memory_space=pltpu.VMEM)
    smem = pl.BlockSpec(memory_space=pltpu.SMEM)
    hbm = pl.BlockSpec(memory_space=pl.ANY)

    def buf(*shape, dtype=bf16):
        return pltpu.VMEM(shape, dtype)

    return pl.pallas_call(
        kernel,
        out_shape=(
            jax.ShapeDtypeStruct((ROWS, FEAT), bf16),
            jax.ShapeDtypeStruct((ROWS, FEAT), bf16),
            jax.ShapeDtypeStruct((FEAT, HID), f32),
            jax.ShapeDtypeStruct((HID, FEAT), f32),
        ),
        in_specs=[vmem, vmem, smem, hbm, hbm],
        out_specs=(vmem, vmem, hbm, hbm),
        scratch_shapes=[
            buf(BLOCK, FEAT, dtype=f32),
            buf(2, NY, NL, BLOCK, CA),
            buf(2, NY, NL, BLOCK, CB),
            buf(2, NY, NL, BLOCK, CA),
            buf(2, NY, NL, BLOCK, CB),
            buf(FEAT, 4 * HID),
            buf(2, 2 * HID, FEAT),
            buf(3, 2, 32, 4 * HID),
            buf(3, 2, 32, 4 * HID),
            buf(2, 32, 4 * HID, dtype=f32),
            buf(NY, 2, 32, 2 * HID),
            buf(NY, 32, 2 * HID),
            buf(2, NY, NL, BLOCK, CA, dtype=f32),
            buf(2, NY, NL, BLOCK, CB, dtype=f32),
            buf(16, NL, BLOCK, CA),
            buf(16, NL, BLOCK, CA),
            buf(2, NL, BLOCK, CA),
            buf(2, 2, BLOCK, CA),
            buf(2, BLOCK, CA),
            buf(6, NY, BLOCK, CB),
            buf(6, NY, BLOCK, CB),
            buf(NY, 2, BLOCK, CB),
            buf(NY - 1, 2, BLOCK, CB),
            buf(NH, 2, BLOCK, CA),
            buf(NH, 2, BLOCK, CB),
            buf(2 * HID, 1024),
            buf(FEAT, HID, dtype=f32),
            buf(HID, FEAT, dtype=f32),
            pltpu.SemaphoreType.DMA((N_SEMS,)),
            pltpu.SemaphoreType.DMA((N_SEMS,)),
            pltpu.SemaphoreType.DMA((4,)),
        ],
        compiler_params=pltpu.CompilerParams(
            collective_id=0, has_side_effects=True, vmem_limit_bytes=48 * 1024 * 1024
        ),
    )(tokens, cotangent, image_lengths, fc1_weight, fc2_weight)


def solution(mesh):
    return jax.shard_map(
        per_device,
        mesh=mesh,
        in_specs=(
            P("tok", "fin"),
            P("tok", "fin"),
            P(),
            P("fin", ("tok", "fout")),
            P(("tok", "fout"), "fin"),
        ),
        out_specs=(
            P("tok", "fin"),
            P("tok", "fin"),
            P("fin", ("tok", "fout")),
            P(("tok", "fout"), "fin"),
        ),
        check_vma=False,
    )
```

time: 1550 us -> 83.9 us (0.05)
  the two profiles are of different devices: /device:TPU:192 before, /device:TPU:2 now
where the time goes in v1:
time: 83.9 us; the launch traced here: 83.6 us
  Pallas kernels  75.8 us (90%)
  local copies, waits for them, and re-layouts  7.09 us (8%)
    pallas_call x1, Pallas kernels, per_device(): pl.pallas_call(kernel, out_shape=(jax.ShapeDtypeStruct((ROWS, FEAT), bf16...  75.8 us
    unnamed x14, local copies, waits for them, and re-layouts  7.09 us

profile of v1, /device:TPU:2, one launch (start us, length us, event | category | flops | bytes accessed | tf_op | source)
XLA Modules:
  0.0 83.6 jit_solution(3812581518728383527)
XLA Ops:
  0.6 0.0 copy-start
  0.6 1.0 %copy-done = bf16[1536,128]{1,0:T(8,128)(2,1)S(1)} copy-done((bf16[1536,128]{1,0:T(8,128)(2,1)S(1)}, bf16[1536,128]{1,0:T(8,128)(2,1)}, u32[]{:S(2)}) %copy-start) | copy-done | bytes 393240
  1.6 0.0 copy-start.1
  1.6 1.0 %copy-done.1 = bf16[128,1536]{1,0:T(8,128)(2,1)S(1)} copy-done((bf16[128,1536]{1,0:T(8,128)(2,1)S(1)}, bf16[128,1536]{1,0:T(8,128)(2,1)}, u32[]{:S(2)}) %copy-start.1) | copy-done | bytes 393240
  2.6 0.0 copy-start.2
  2.6 0.7 copy-done.2
  3.4 0.0 copy-start.3
  3.4 0.7 copy-done.3
  4.1 0.0 copy-start.4
  4.1 0.7 copy-done.4
  4.8 75.8 %shard_map.84 = (bf16[6,1536]{1,0:T(8,128)(2,1)S(1)}, bf16[6,1536]{1,0:T(8,128)(2,1)S(1)}, f32[1536,128]{1,0:T(8,128)S(1)}, f32[128,1536]{1,0:T(8,128)S(1)}) custom-call(bf16[6,1536]{1,0:T(8,128)(2,1)S(1)} %copy-done.2, bf16[6,1536]{1,0:T(8,128)(2,1)S(1)} %copy-done.3, s32[16]{0:T(128)S(1)} %copy-done.4, bf16[1536,128]{1,0:T(8,128)(2,1)S(1)} %copy-done, ...), custom_call_target="tpu_custom_call" | custom-call | tf_op jit(solution)/shard_map/pallas_call | solution.py:372
  80.6 0.6 copy.13
  81.2 0.6 copy.14
  81.8 0.9 %copy.15 = f32[1536,128]{1,0:T(8,128)} copy(f32[1536,128]{1,0:T(8,128)S(1)} %get-tuple-element.10) | data formatting | bytes 1572864
  82.7 0.9 %copy.16 = f32[128,1536]{1,0:T(8,128)} copy(f32[128,1536]{1,0:T(8,128)S(1)} %get-tuple-element.11) | data formatting | bytes 1572864
Async XLA Ops:
  0.6 1.0 %copy-start = (bf16[1536,128]{1,0:T(8,128)(2,1)S(1)}, bf16[1536,128]{1,0:T(8,128)(2,1)}, u32[]{:S(2)}) copy-start(bf16[1536,128]{1,0:T(8,128)(2,1)} %w1_ref.1) | copy-start | bytes 1179652
  1.6 1.0 %copy-start.1 = (bf16[128,1536]{1,0:T(8,128)(2,1)S(1)}, bf16[128,1536]{1,0:T(8,128)(2,1)}, u32[]{:S(2)}) copy-start(bf16[128,1536]{1,0:T(8,128)(2,1)} %w2_ref.1) | copy-start | bytes 1179652
  2.6 0.7 copy-start.2
  3.4 0.7 copy-start.3
  4.1 0.7 copy-start.4

commit v2 on v0

v2 whole, which is shorter than its diff:
```python
import jax
import jax.numpy as jnp
from jax import lax
from jax.experimental import pallas as pl
from jax.experimental.pallas import tpu as pltpu
from jax.sharding import PartitionSpec as P

inv_root_two = 0.7071067811865476
inv_root_two_pi = 0.3989422804014327

NX, NY, NL, NH = 4, 8, 4, 3
NZ = NL * NH
ROWS = 6
BLOCK = 16
FEAT = 1536
HID = 128
LONGEST = 48
TAIL = FEAT // 4
FOLD = FEAT - TAIL
WA = 512
WB = FOLD - WA
FAR = (4, 3, 5, 2, 6, 1, 7, 0)
N_SEMS = 80

bf16, f32 = jnp.bfloat16, jnp.float32


def place(d):
    return FAR.index(d % NY)


def sublane(v):
    return lax.broadcasted_iota(jnp.int32, v.shape, 1)


def fold(v):
    w = v.shape[2] // 4
    tail = v[:, :, 3 * w :]
    row = sublane(tail)
    segments = []
    for i in range(3):
        low = jnp.broadcast_to(tail[:, i : i + 1], tail.shape)
        high = jnp.broadcast_to(tail[:, 3 + i : 4 + i], tail.shape)
        main = v[:, :, i * w : (i + 1) * w]
        segments.append(jnp.where(row == 6, low, jnp.where(row == 7, high, main)))
    return jnp.concatenate(segments, axis=2)


def unfold(v):
    w = v.shape[2] // 3
    segments = [v[:, :, i * w : (i + 1) * w] for i in range(3)]
    row = sublane(segments[0])
    tail = jnp.zeros_like(segments[0])
    for i in range(6):
        source = segments[i % 3][:, 6 + i // 3 : 7 + i // 3]
        tail = jnp.where(row == i, jnp.broadcast_to(source, tail.shape), tail)
    real = [jnp.where(row < 6, segment, 0.0) for segment in segments]
    return jnp.concatenate(real + [tail], axis=2)


def kernel(
    tok_hbm, cot_hbm, len_hbm, w1_ref, w2_ref,
    out_ref, gtok_ref, g1_ref, g2_ref,
    tok_ref, cot_ref, len_ref, xb, pm,
    xa, xbk, xt, xsa, xsb, xst, wc, wt,
    rf, rs, rr, ag, ags,
    ysa, ysb, ray, rza, saz, rbz, sby, rby, vha, vhb,
    mt, g1v, g2v,
    send_sem, recv_sem, local_sem,
):
    t = lax.axis_index("tok")
    x = lax.axis_index("fin")
    f = lax.axis_index("fout")
    c = lax.rem(t, 2)
    y = lax.rem(lax.div(t, 2), NY)
    zl = lax.div(t, 2 * NY)
    z = f * NL + zl

    def on_y(d):
        return {"tok": (zl * NY + lax.rem(y + d + NY, NY)) * 2 + c}

    def on_z(d):
        far = lax.rem(z + d + NZ, NZ)
        return {
            "tok": (lax.rem(far, NL) * NY + y) * 2 + c,
            "fout": lax.div(far, NL),
        }

    def on_x(d):
        return {"fin": lax.rem(x + d, NX)}

    sibling = {"tok": t + 1 - 2 * c}

    sent = []

    def send(src, dst, device):
        i = len(sent)
        copy = pltpu.make_async_remote_copy(
            src_ref=src, dst_ref=dst,
            send_sem=send_sem.at[i], recv_sem=recv_sem.at[i],
            device_id=device, device_id_type=pl.DeviceIdType.MESH,
        )
        copy.start()
        sent.append(copy)
        return copy

    def arrived(copies):
        for copy in copies:
            copy.wait_recv()

    small = [
        pltpu.make_async_copy(src, dst, local_sem.at[4 + i])
        for i, (src, dst) in enumerate(
            ((len_hbm, len_ref), (cot_hbm, cot_ref), (tok_hbm, tok_ref))
        )
    ]
    for copy in small:
        copy.start()
    own_w1 = pltpu.make_async_copy(w1_ref, wc.at[:, 0:HID], local_sem.at[0])
    own_w2 = pltpu.make_async_copy(w2_ref, wt.at[0, 0:HID], local_sem.at[1])
    own_w1.start()
    own_w2.start()

    barrier = pltpu.get_barrier_semaphore()
    partners = (
        [sibling]
        + [on_x(d) for d in (1, 2, 3)]
        + [on_y(d) for d in (1, 2, 3, 4, 5, 6, 7)]
        + [on_z(d) for d in (1, -1, 2, -2, 4, -4)]
    )
    for device in partners:
        pl.semaphore_signal(
            barrier, inc=1, device_id=device, device_id_type=pl.DeviceIdType.MESH
        )

    for copy in small:
        copy.wait()
    position = t * ROWS + lax.broadcasted_iota(jnp.int32, (8, 128), 0)
    span = jnp.zeros((8, 128), jnp.int32)
    start = jnp.int32(0)
    for i in range(16):
        length = len_ref[i]
        end = start + length
        span = jnp.where((position >= start) & (position < end), length, span)
        start = end
    ratio = f32(LONGEST) / jnp.maximum(span, 1).astype(f32)
    scale = jnp.where(span > 0, jnp.sqrt(ratio), f32(0.0))
    scale = jnp.concatenate([scale] * (FEAT // 128), axis=1)[0:ROWS]
    xb[...] = jnp.zeros_like(xb)
    xb[0:ROWS] = tok_ref[...].astype(f32)
    xb[8 : 8 + ROWS] = cot_ref[...].astype(f32) * scale
    block = fold(xb[...].reshape(2, 8, FEAT)).reshape(BLOCK, FOLD).astype(bf16)
    home = place(0)
    xa[home, 0] = block[:, 0:WA]
    xbk[home, 0] = block[:, WA:]

    pl.semaphore_wait(barrier, len(partners))

    ga_z = [send(xa.at[home, 0], xa.at[home, -d % NL], on_z(d)) for d in (1, -1)]
    for d, cols in ((2, slice(0, WA // 2)), (-2, slice(WA // 2, WA))):
        ga_z.append(send(xa.at[home, 0, :, cols], xa.at[home, 2, :, cols], on_z(d)))
    gb_y = [
        send(xbk.at[home, 0], xbk.at[place(-d), 0], on_y(d)) for d in FAR[:-1]
    ]
    sib_w1 = send(w1_ref, wc.at[:, HID : 2 * HID], sibling)
    sib_w2 = send(w2_ref, wt.at[0, HID : 2 * HID], sibling)

    r = lax.broadcasted_iota(jnp.int32, (128, 384), 0)
    q = lax.broadcasted_iota(jnp.int32, (128, 384), 1)
    i = lax.rem(r, 8)
    late = jnp.where(i >= 3, 1, 0)
    spot = (i - 3 * late) * 128 + (r - i) + 6 + late
    pm[...] = jnp.where((i < 6) & (q == spot), f32(1.0), f32(0.0)).astype(bf16)
    own_w1.wait()
    own_w2.wait()
    wc[:, 2 * HID : 3 * HID] = wt[0, 0:HID].T
    wt[1, 0:HID] = wc[:, 0:HID].T

    arrived(ga_z)
    ga_y = [send(xa.at[home], xa.at[place(-d)], on_y(d)) for d in FAR[:-1]]
    arrived(gb_y)
    gb_z = [send(xbk.at[:, 0], xbk.at[:, -d % NL], on_z(d)) for d in (1, -1)]
    for d, js in ((2, slice(0, 4)), (-2, slice(4, 8))):
        gb_z.append(send(xbk.at[js, 0], xbk.at[js, 2], on_z(d)))
    arrived([sib_w1, sib_w2])
    wc[:, 3 * HID : 4 * HID] = wt[0, HID : 2 * HID].T
    wt[1, HID : 2 * HID] = wc[:, HID : 2 * HID].T
    arrived(ga_y)
    arrived(gb_z)

    def tails(dst, part_a, part_b, g):
        js = slice(2 * g, 2 * g + 2)
        whole = jnp.concatenate(
            [part_a[js].reshape(128, WA), part_b[js].reshape(128, WB)], axis=1
        )
        stacked = jnp.concatenate(
            [whole[:, i * TAIL : (i + 1) * TAIL] for i in range(3)], axis=0
        )
        value = jnp.dot(pm[...], stacked, preferred_element_type=f32)
        dst[js] = value.astype(bf16).reshape(2, NL, BLOCK, TAIL)

    def partial(h):
        tails(xt, xa, xbk, 2 * h)
        tails(xt, xa, xbk, 2 * h + 1)
        js = slice(4 * h, 4 * h + 4)
        lhs = jnp.concatenate(
            [
                xa[js].reshape(256, WA),
                xbk[js].reshape(256, WB),
                xt[js].reshape(256, TAIL),
            ],
            axis=1,
        )
        pre = jnp.dot(lhs, wc[:, 0 : 2 * HID], preferred_element_type=f32)
        back = jnp.dot(lhs, wc[:, 2 * HID : 4 * HID], preferred_element_type=f32)
        pre = pre.reshape(16, 2, 8, 2 * HID)[:, 0]
        back = back.reshape(16, 2, 8, 2 * HID)[:, 1]
        value = fold(jnp.concatenate([pre, back], axis=2)).reshape(4, 32, 3 * HID)
        rf[js] = value
        rs[js] = value.astype(bf16)

    x_in = {}
    for h in range(2):
        partial(h)
        x_in[h] = []
        for d in (2, 1, 3):
            j = 4 * h + lax.rem(x + d, NX)
            x_in[h].append(send(rs.at[j], rr.at[h, d - 1], on_x(d)))
    xs = [send(xa, xsa, sibling), send(xbk, xsb, sibling)]
    x_out = {}
    for h in range(2):
        arrived(x_in[h])
        mine = 4 * h + x
        total = rf[mine]
        for d in range(3):
            total = total + rr[h, d].astype(f32)
        total = unfold(total.reshape(4, 8, 3 * HID))
        pre, back = total[:, :, 0 : 2 * HID], total[:, :, 2 * HID : 4 * HID]
        cdf = 0.5 * (1.0 + lax.erf(pre * inv_root_two))
        density = jnp.exp(-0.5 * pre * pre) * inv_root_two_pi
        act = pre * cdf
        gp = back * (cdf + pre * density)
        value = jnp.concatenate(
            [act[:, :, 0:HID], gp[:, :, 0:HID], act[:, :, HID:], gp[:, :, HID:]],
            axis=2,
        )
        ag[mine] = fold(value).reshape(32, 3 * HID).astype(bf16)
        x_out[h] = [send(ag.at[mine], ag.at[mine], on_x(d)) for d in (2, 1, 3)]

    def outputs(h):
        js = slice(4 * h, 4 * h + 4)
        u = unfold(ag[js].astype(f32).reshape(16, 8, 3 * HID)).reshape(128, 4 * HID)
        u = u.astype(bf16)
        act2 = jnp.concatenate([u[:, 0:HID], u[:, 2 * HID : 3 * HID]], axis=1)
        gp2 = jnp.concatenate([u[:, HID : 2 * HID], u[:, 3 * HID :]], axis=1)
        fwd = jnp.dot(act2, wt[0], preferred_element_type=f32)
        bwd = jnp.dot(gp2, wt[1], preferred_element_type=f32)
        fwd = fold(fwd.reshape(16, 8, FEAT))
        bwd = fold(bwd.reshape(16, 8, FEAT))
        value = jnp.concatenate([fwd, bwd], axis=1).astype(bf16)
        ysa[js] = value[:, :, 0:WA].reshape(4, NL, BLOCK, WA)
        ysb[js] = value[:, :, WA:].reshape(4, NL, BLOCK, WB)

    ra_y, rb_z = [], []
    for h in range(2):
        arrived(x_out[h])
        outputs(h)
        js = slice(4 * h, 4 * h + 4)
        d = (2, -2)[h]
        rb_z.append(send(ysb.at[js, 2], rbz.at[2, js], on_z(d)))
        for w, d in enumerate((1, -1)):
            rb_z.append(send(ysb.at[js, d % NL], rbz.at[w, js], on_z(d)))
        for j in range(4 * h, min(4 * h + 4, NY - 1)):
            ra_y.append(send(ysa.at[j], ray.at[j], on_y(FAR[j])))

    ag_sib = send(ag, ags, sibling)

    def spread(v, lanes):
        v = unfold(v.astype(f32).reshape(32, 8, 3 * HID))[:, :, lanes]
        none = jnp.zeros((32, 8, HID), f32)
        first = jnp.concatenate([v[:, :, HID:], none], axis=2)
        second = jnp.concatenate([none, v[:, :, 0:HID]], axis=2)
        both = jnp.concatenate([first, second], axis=1)
        return both.reshape(512, 2 * HID).astype(bf16)

    mt[:, 0:512] = spread(ag[...], slice(0, 2 * HID)).T
    arrived(xs)
    for g in range(4):
        tails(xst, xsa, xsb, g)
    arrived([ag_sib])
    mt[:, 512:1024] = spread(ags[...], slice(2 * HID, 4 * HID)).T

    def weight_grads(src, src_sib, width, first):
        for n in range(0, width, 256):
            lanes = slice(n, min(n + 256, width))
            size = lanes.stop - lanes.start
            lhs = src[:, :, :, lanes].reshape(512, size)
            rhs = src_sib[:, :, :, lanes].reshape(512, size)
            g = jnp.dot(mt[:, 0:512], lhs, preferred_element_type=f32)
            g = g + jnp.dot(mt[:, 512:1024], rhs, preferred_element_type=f32)
            cols = slice(first + n, first + n + size)
            g1v[cols, :] = g[0:HID].T
            g2v[:, cols] = g[HID:]

    weight_grads(xa, xsa, WA, 0)

    arrived(rb_z)
    value = ysb[:, 0].astype(f32)
    for w in range(3):
        value = value + rbz[w].astype(f32)
    sby[...] = value.astype(bf16)
    rb_y = [send(sby.at[j], rby.at[j], on_y(FAR[j])) for j in range(NY - 1)]
    weight_grads(xbk, xsb, WB, WA)

    arrived(ra_y)
    value = ysa[home].astype(f32)
    for j in range(NY - 1):
        value = value + ray[j].astype(f32)
    saz[...] = value.astype(bf16)
    ra_z = [send(saz.at[d % NL], rza.at[w], on_z(d)) for w, d in enumerate((1, -1))]
    for d, cols in ((2, slice(0, WA // 2)), (-2, slice(WA // 2, WA))):
        ra_z.append(send(saz.at[2, :, cols], rza.at[2, :, cols], on_z(d)))
    weight_grads(xt, xst, TAIL, FOLD)
    out_g1 = pltpu.make_async_copy(g1v, g1_ref, local_sem.at[2])
    out_g2 = pltpu.make_async_copy(g2v, g2_ref, local_sem.at[3])
    out_g1.start()
    out_g2.start()

    arrived(rb_y)
    value = sby[home].astype(f32)
    for j in range(NY - 1):
        value = value + rby[j].astype(f32)
    vhb[f] = value.astype(bf16)
    last = [send(vhb.at[f], vhb.at[f], on_z(d)) for d in (4, -4)]
    arrived(ra_z)
    value = saz[0].astype(f32)
    for w in range(3):
        value = value + rza[w].astype(f32)
    vha[f] = value.astype(bf16)
    last += [send(vha.at[f], vha.at[f], on_z(d)) for d in (4, -4)]
    arrived(last)
    value = jnp.concatenate(
        [
            v[0].astype(f32) + v[1].astype(f32) + v[2].astype(f32)
            for v in (vha, vhb)
        ],
        axis=1,
    )
    value = unfold(value.reshape(2, 8, FOLD))
    out_ref[...] = value[0, 0:ROWS].astype(bf16)
    gtok_ref[...] = value[1, 0:ROWS].astype(bf16)

    out_g1.wait()
    out_g2.wait()
    for copy in sent:
        copy.wait_send()


def per_device(tokens, cotangent, image_lengths, fc1_weight, fc2_weight):
    vmem = pl.BlockSpec(memory_space=pltpu.VMEM)
    hbm = pl.BlockSpec(memory_space=pl.ANY)

    def buf(*shape, dtype=bf16):
        return pltpu.VMEM(shape, dtype)

    return pl.pallas_call(
        kernel,
        out_shape=(
            jax.ShapeDtypeStruct((ROWS, FEAT), bf16),
            jax.ShapeDtypeStruct((ROWS, FEAT), bf16),
            jax.ShapeDtypeStruct((FEAT, HID), f32),
            jax.ShapeDtypeStruct((HID, FEAT), f32),
        ),
        in_specs=[hbm] * 5,
        out_specs=(vmem, vmem, hbm, hbm),
        scratch_shapes=[
            buf(ROWS, FEAT),
            buf(ROWS, FEAT),
            pltpu.SMEM((16,), jnp.int32),
            buf(BLOCK, FEAT, dtype=f32),
            buf(128, 384),
            buf(NY, NL, BLOCK, WA),
            buf(NY, NL, BLOCK, WB),
            buf(NY, NL, BLOCK, TAIL),
            buf(NY, NL, BLOCK, WA),
            buf(NY, NL, BLOCK, WB),
            buf(NY, NL, BLOCK, TAIL),
            buf(FEAT, 4 * HID),
            buf(2, 2 * HID, FEAT),
            buf(NY, 32, 3 * HID, dtype=f32),
            buf(NY, 32, 3 * HID),
            buf(2, 3, 32, 3 * HID),
            buf(NY, 32, 3 * HID),
            buf(NY, 32, 3 * HID),
            buf(NY, NL, BLOCK, WA),
            buf(NY, NL, BLOCK, WB),
            buf(NY - 1, NL, BLOCK, WA),
            buf(3, BLOCK, WA),
            buf(NL, BLOCK, WA),
            buf(3, NY, BLOCK, WB),
            buf(NY, BLOCK, WB),
            buf(NY - 1, BLOCK, WB),
            buf(NH, BLOCK, WA),
            buf(NH, BLOCK, WB),
            buf(2 * HID, 1024),
            buf(FEAT, HID, dtype=f32),
            buf(HID, FEAT, dtype=f32),
            pltpu.SemaphoreType.DMA((N_SEMS,)),
            pltpu.SemaphoreType.DMA((N_SEMS,)),
            pltpu.SemaphoreType.DMA((8,)),
        ],
        compiler_params=pltpu.CompilerParams(
            collective_id=0, has_side_effects=True, vmem_limit_bytes=60 * 1024 * 1024
        ),
    )(tokens, cotangent, image_lengths, fc1_weight, fc2_weight)


def solution(mesh):
    return jax.shard_map(
        per_device,
        mesh=mesh,
        in_specs=(
            P("tok", "fin"),
            P("tok", "fin"),
            P(),
            P("fin", ("tok", "fout")),
            P(("tok", "fout"), "fin"),
        ),
        out_specs=(
            P("tok", "fin"),
            P("tok", "fin"),
            P("fin", ("tok", "fout")),
            P(("tok", "fout"), "fin"),
        ),
        check_vma=False,
    )
```

time: 1550 us -> 73.2 us (0.05)
  the two profiles are of different devices: /device:TPU:192 before, /device:TPU:16 now
where the time goes in v2:
time: 73.2 us; the launch traced here: 72.9 us
  Pallas kernels  67.3 us (92%)
  local copies, waits for them, and re-layouts  4.98 us (7%)
    pallas_call x1, Pallas kernels, per_device(): pl.pallas_call(kernel, out_shape=(jax.ShapeDtypeStruct((ROWS, FEAT), bf16...  67.3 us
    unnamed x8, local copies, waits for them, and re-layouts  4.98 us

profile of v2, /device:TPU:16, one launch (start us, length us, event | category | flops | bytes accessed | tf_op | source)
XLA Modules:
  0.0 72.9 jit_solution(3858209844084523012)
XLA Ops:
  0.6 67.3 %shard_map.84 = (bf16[6,1536]{1,0:T(8,128)(2,1)}, bf16[6,1536]{1,0:T(8,128)(2,1)}, f32[1536,128]{1,0:T(8,128)}, f32[128,1536]{1,0:T(8,128)}) custom-call(bf16[6,1536]{1,0:T(8,128)(2,1)} %tok_hbm.1, bf16[6,1536]{1,0:T(8,128)(2,1)} %cot_hbm.1, s32[16]{0:T(128)} %len_hbm.1, bf16[1536,128]{1,0:T(8,128)(2,1)} %w1_ref.1, bf16[128,1536]{1,0:T(8,128)(2,1)} %w2_ref.1), custom_call_target="tpu_custom_call" | custom-call | tf_op jit(solution)/shard_map/pallas_call | solution.py:366
  67.9 0.0 copy-start.1
  67.9 1.4 %copy.13 = bf16[6,1536]{1,0:T(8,128)(2,1)} copy(bf16[6,1536]{1,0:T(8,128)(2,1)} %get-tuple-element.8) | data formatting | bytes 36864
  69.3 0.0 copy-done.1
  69.3 0.6 copy.14
  69.9 0.0 copy-start
  69.9 2.1 %copy.15 = f32[1536,128]{1,0:T(8,128)} copy(f32[1536,128]{1,0:T(8,128)} %get-tuple-element.10) | data formatting | bytes 1572864
  72.0 0.0 copy-done
  72.0 0.9 %copy.16 = f32[128,1536]{1,0:T(8,128)} copy(f32[128,1536]{1,0:T(8,128)S(1)} %copy-done) | data formatting | bytes 1572864
Async XLA Ops:
  67.9 1.4 %copy-start.1 = (bf16[6,1536]{1,0:T(8,128)(2,1)S(1)}, bf16[6,1536]{1,0:T(8,128)(2,1)}, u32[]{:S(2)}) copy-start(bf16[6,1536]{1,0:T(8,128)(2,1)} %get-tuple-element.9) | copy-start | bytes 55300
  69.9 2.1 %copy-start = (f32[128,1536]{1,0:T(8,128)S(1)}, f32[128,1536]{1,0:T(8,128)}, u32[]{:S(2)}) copy-start(f32[128,1536]{1,0:T(8,128)} %get-tuple-element.11) | copy-start | bytes 2359300

commit v3 on v2

--- a/solution.py
+++ b/solution.py
@@ -19,6 +19,7 @@
 FOLD = FEAT - TAIL
 WA = 512
 WB = FOLD - WA
+WC = WA // 2
 FAR = (4, 3, 5, 2, 6, 1, 7, 0)
 N_SEMS = 80
 
@@ -60,12 +61,12 @@
 
 def kernel(
     tok_hbm, cot_hbm, len_hbm, w1_ref, w2_ref,
-    out_ref, gtok_ref, g1_ref, g2_ref,
+    out_ref, gtok_ref, g1v, g2v,
     tok_ref, cot_ref, len_ref, xb, pm,
     xa, xbk, xt, xsa, xsb, xst, wc, wt,
     rf, rs, rr, ag, ags,
-    ysa, ysb, ray, rza, saz, rbz, sby, rby, vha, vhb,
-    mt, g1v, g2v,
+    ysa, ysb, rel, rel2, ray, rza, saz, rbz, sby, rby, vha, vhb,
+    mt,
     send_sem, recv_sem, local_sem,
 ):
     t = lax.axis_index("tok")
@@ -157,7 +158,7 @@
     pl.semaphore_wait(barrier, len(partners))
 
     ga_z = [send(xa.at[home, 0], xa.at[home, -d % NL], on_z(d)) for d in (1, -1)]
-    for d, cols in ((2, slice(0, WA // 2)), (-2, slice(WA // 2, WA))):
+    for d, cols in ((2, slice(0, WC)), (-2, slice(WC, WA))):
         ga_z.append(send(xa.at[home, 0, :, cols], xa.at[home, 2, :, cols], on_z(d)))
     gb_y = [
         send(xbk.at[home, 0], xbk.at[place(-d), 0], on_y(d)) for d in FAR[:-1]
@@ -177,15 +178,23 @@
     wt[1, 0:HID] = wc[:, 0:HID].T
 
     arrived(ga_z)
-    ga_y = [send(xa.at[home], xa.at[place(-d)], on_y(d)) for d in FAR[:-1]]
+    ga_y = {d: send(xa.at[home], xa.at[place(-d)], on_y(d)) for d in (2, -2, 1, -1)}
     arrived(gb_y)
     gb_z = [send(xbk.at[:, 0], xbk.at[:, -d % NL], on_z(d)) for d in (1, -1)]
     for d, js in ((2, slice(0, 4)), (-2, slice(4, 8))):
         gb_z.append(send(xbk.at[js, 0], xbk.at[js, 2], on_z(d)))
+    ga_far = []
+    for way, ks in ((1, slice(0, 2)), (-1, slice(2, 4))):
+        arrived([ga_y[2 * way]])
+        group = place(-2 * way)
+        ga_far.append(
+            send(xa.at[group, ks], xa.at[place(4), ks], on_y(2 * way))
+        )
+        ga_far.append(send(xa.at[group], xa.at[place(-3 * way)], on_y(way)))
     arrived([sib_w1, sib_w2])
     wc[:, 3 * HID : 4 * HID] = wt[0, HID : 2 * HID].T
     wt[1, HID : 2 * HID] = wc[:, HID : 2 * HID].T
-    arrived(ga_y)
+    arrived([ga_y[1], ga_y[-1]] + ga_far)
     arrived(gb_z)
 
     def tails(dst, part_a, part_b, g):
@@ -261,7 +270,7 @@
         ysa[js] = value[:, :, 0:WA].reshape(4, NL, BLOCK, WA)
         ysb[js] = value[:, :, WA:].reshape(4, NL, BLOCK, WB)
 
-    ra_y, rb_z = [], []
+    ra_y, rb_z, relay = [], [], []
     for h in range(2):
         arrived(x_out[h])
         outputs(h)
@@ -270,8 +279,23 @@
         rb_z.append(send(ysb.at[js, 2], rbz.at[2, js], on_z(d)))
         for w, d in enumerate((1, -1)):
             rb_z.append(send(ysb.at[js, d % NL], rbz.at[w, js], on_z(d)))
-        for j in range(4 * h, min(4 * h + 4, NY - 1)):
-            ra_y.append(send(ysa.at[j], ray.at[j], on_y(FAR[j])))
+        for way, ks in ((1, slice(0, 2)), (-1, slice(2, 4))):
+            w = (1 - way) // 2
+            if h == 0:
+                relay.append(send(ysa.at[place(3 * way)], rel.at[w], on_y(way)))
+                far = send(ysa.at[place(4), ks], rel.at[2 + w, ks], on_y(2 * way))
+                relay.append(far)
+            else:
+                ra_y.append(send(ysa.at[place(way)], ray.at[w], on_y(way)))
+
+    arrived(relay)
+    for way, ks in ((1, slice(0, 2)), (-1, slice(2, 4))):
+        w = (1 - way) // 2
+        value = ysa[place(2 * way)].astype(f32) + rel[w].astype(f32)
+        extra = rel[2 + w, ks].astype(f32)
+        rel2[w] = value.astype(bf16)
+        rel2[w, ks] = (value[ks] + extra).astype(bf16)
+        ra_y.append(send(rel2.at[w], ray.at[2 + w], on_y(2 * way)))
 
     ag_sib = send(ag, ags, sibling)
 
@@ -314,17 +338,13 @@
 
     arrived(ra_y)
     value = ysa[home].astype(f32)
-    for j in range(NY - 1):
+    for j in range(4):
         value = value + ray[j].astype(f32)
     saz[...] = value.astype(bf16)
     ra_z = [send(saz.at[d % NL], rza.at[w], on_z(d)) for w, d in enumerate((1, -1))]
-    for d, cols in ((2, slice(0, WA // 2)), (-2, slice(WA // 2, WA))):
+    for d, cols in ((2, slice(0, WC)), (-2, slice(WC, WA))):
         ra_z.append(send(saz.at[2, :, cols], rza.at[2, :, cols], on_z(d)))
     weight_grads(xt, xst, TAIL, FOLD)
-    out_g1 = pltpu.make_async_copy(g1v, g1_ref, local_sem.at[2])
-    out_g2 = pltpu.make_async_copy(g2v, g2_ref, local_sem.at[3])
-    out_g1.start()
-    out_g2.start()
 
     arrived(rb_y)
     value = sby[home].astype(f32)
@@ -350,10 +370,17 @@
     out_ref[...] = value[0, 0:ROWS].astype(bf16)
     gtok_ref[...] = value[1, 0:ROWS].astype(bf16)
 
-    out_g1.wait()
-    out_g2.wait()
     for copy in sent:
         copy.wait_send()
+
+
+def write_out(*refs):
+    sem = refs[8]
+    copies = [pltpu.make_async_copy(refs[i], refs[4 + i], sem.at[i]) for i in range(4)]
+    for copy in copies:
+        copy.start()
+    for copy in copies:
+        copy.wait()
 
 
 def per_device(tokens, cotangent, image_lengths, fc1_weight, fc2_weight):
@@ -363,16 +390,21 @@
     def buf(*shape, dtype=bf16):
         return pltpu.VMEM(shape, dtype)
 
-    return pl.pallas_call(
+    shapes = (
+        ((ROWS, FEAT), bf16),
+        ((ROWS, FEAT), bf16),
+        ((FEAT, HID), f32),
+        ((HID, FEAT), f32),
+    )
+    arguments = [
+        pltpu.with_memory_space_constraint(a, pltpu.HBM)
+        for a in (tokens, cotangent, image_lengths, fc1_weight, fc2_weight)
+    ]
+    results = pl.pallas_call(
         kernel,
-        out_shape=(
-            jax.ShapeDtypeStruct((ROWS, FEAT), bf16),
-            jax.ShapeDtypeStruct((ROWS, FEAT), bf16),
-            jax.ShapeDtypeStruct((FEAT, HID), f32),
-            jax.ShapeDtypeStruct((HID, FEAT), f32),
-        ),
+        out_shape=tuple(pltpu.VMEM(*shape) for shape in shapes),
         in_specs=[hbm] * 5,
-        out_specs=(vmem, vmem, hbm, hbm),
+        out_specs=(vmem,) * 4,
         scratch_shapes=[
             buf(ROWS, FEAT),
             buf(ROWS, FEAT),
@@ -394,7 +426,9 @@
             buf(NY, 32, 3 * HID),
             buf(NY, NL, BLOCK, WA),
             buf(NY, NL, BLOCK, WB),
-            buf(NY - 1, NL, BLOCK, WA),
+            buf(4, NL, BLOCK, WA),
+            buf(2, NL, BLOCK, WA),
+            buf(4, NL, BLOCK, WA),
             buf(3, BLOCK, WA),
             buf(NL, BLOCK, WA),
             buf(3, NY, BLOCK, WB),
@@ -403,16 +437,22 @@
             buf(NH, BLOCK, WA),
             buf(NH, BLOCK, WB),
             buf(2 * HID, 1024),
-            buf(FEAT, HID, dtype=f32),
-            buf(HID, FEAT, dtype=f32),
             pltpu.SemaphoreType.DMA((N_SEMS,)),
             pltpu.SemaphoreType.DMA((N_SEMS,)),
             pltpu.SemaphoreType.DMA((8,)),
         ],
         compiler_params=pltpu.CompilerParams(
-            collective_id=0, has_side_effects=True, vmem_limit_bytes=60 * 1024 * 1024
+            collective_id=0, has_side_effects=True, vmem_limit_bytes=44 * 1024 * 1024
         ),
-    )(tokens, cotangent, image_lengths, fc1_weight, fc2_weight)
+    )(*arguments)
+    return pl.pallas_call(
+        write_out,
+        out_shape=tuple(jax.ShapeDtypeStruct(*shape) for shape in shapes),
+        in_specs=[vmem] * 4,
+        out_specs=(hbm,) * 4,
+        scratch_shapes=[pltpu.SemaphoreType.DMA((4,))],
+        compiler_params=pltpu.CompilerParams(vmem_limit_bytes=4 * 1024 * 1024),
+    )(*results)
 
 
 def solution(mesh):

time: 73.2 us -> 64.6 us (0.88)
  the two profiles are of different devices: /device:TPU:16 before, /device:TPU:8 now
where the time goes in v3:
time: 64.6 us; the launch traced here: 64.5 us
  Pallas kernels  63.8 us (99%)
    pallas_call x1, Pallas kernels, per_device(): pl.pallas_call(kernel, out_shape=tuple((pltpu.VMEM(*shape) for shape in s...  62.6 us

profile of v3, /device:TPU:8, one launch (start us, length us, event | category | flops | bytes accessed | tf_op | source)
XLA Modules:
  0.0 64.5 jit_solution(7120972369028047040)
XLA Ops:
  0.6 62.6 %shard_map.84 = (bf16[6,1536]{1,0:T(8,128)(2,1)S(1)}, bf16[6,1536]{1,0:T(8,128)(2,1)S(1)}, f32[1536,128]{1,0:T(8,128)S(1)}, f32[128,1536]{1,0:T(8,128)S(1)}) custom-call(bf16[6,1536]{1,0:T(8,128)(2,1)} %tok_hbm.1, bf16[6,1536]{1,0:T(8,128)(2,1)} %cot_hbm.1, s32[16]{0:T(128)} %len_hbm.1, bf16[1536,128]{1,0:T(8,128)(2,1)} %w1_ref.1, bf16[128,1536]{1,0:T(8,128)(2,1)} %w2_ref.1), custom_call_target="tpu_custom_call" | custom-call | tf_op jit(solution)/shard_map/pallas_call | solution.py:403
  63.3 1.2 %shard_map.85 = (bf16[6,1536]{1,0:T(8,128)(2,1)}, bf16[6,1536]{1,0:T(8,128)(2,1)}, f32[1536,128]{1,0:T(8,128)}, f32[128,1536]{1,0:T(8,128)}) custom-call(bf16[6,1536]{1,0:T(8,128)(2,1)S(1)} %get-tuple-element.8.refs_0_, bf16[6,1536]{1,0:T(8,128)(2,1)S(1)} %get-tuple-element.9.refs_1_, f32[1536,128]{1,0:T(8,128)S(1)} %get-tuple-element.10.refs_2_, ...), custom_call_target="tpu_custom_call" | custom-call | tf_op jit(solution)/shard_map/pallas_call | solution.py:448

commit v4 on v3

--- a/solution.py
+++ b/solution.py
@@ -19,7 +19,10 @@
 FOLD = FEAT - TAIL
 WA = 512
 WB = FOLD - WA
-WC = WA // 2
+WC = 256
+RA = 384
+RB = FOLD - RA
+RC = 128
 FAR = (4, 3, 5, 2, 6, 1, 7, 0)
 N_SEMS = 80
 
@@ -65,7 +68,7 @@
     tok_ref, cot_ref, len_ref, xb, pm,
     xa, xbk, xt, xsa, xsb, xst, wc, wt,
     rf, rs, rr, ag, ags,
-    ysa, ysb, rel, rel2, ray, rza, saz, rbz, sby, rby, vha, vhb,
+    ysa, ysb, ray, rza, saz, rbz, sby, rby, vha, vhb,
     mt,
     send_sem, recv_sem, local_sem,
 ):
@@ -160,11 +163,10 @@
     ga_z = [send(xa.at[home, 0], xa.at[home, -d % NL], on_z(d)) for d in (1, -1)]
     for d, cols in ((2, slice(0, WC)), (-2, slice(WC, WA))):
         ga_z.append(send(xa.at[home, 0, :, cols], xa.at[home, 2, :, cols], on_z(d)))
-    gb_y = [
-        send(xbk.at[home, 0], xbk.at[place(-d), 0], on_y(d)) for d in FAR[:-1]
-    ]
-    sib_w1 = send(w1_ref, wc.at[:, HID : 2 * HID], sibling)
-    sib_w2 = send(w2_ref, wt.at[0, HID : 2 * HID], sibling)
+    gb_y = {
+        place(-d): send(xbk.at[home, 0], xbk.at[place(-d), 0], on_y(d))
+        for d in (2, 1, -1, -2, 4, 3, -3)
+    }
 
     r = lax.broadcasted_iota(jnp.int32, (128, 384), 0)
     q = lax.broadcasted_iota(jnp.int32, (128, 384), 1)
@@ -179,10 +181,13 @@
 
     arrived(ga_z)
     ga_y = {d: send(xa.at[home], xa.at[place(-d)], on_y(d)) for d in (2, -2, 1, -1)}
-    arrived(gb_y)
-    gb_z = [send(xbk.at[:, 0], xbk.at[:, -d % NL], on_z(d)) for d in (1, -1)]
-    for d, js in ((2, slice(0, 4)), (-2, slice(4, 8))):
-        gb_z.append(send(xbk.at[js, 0], xbk.at[js, 2], on_z(d)))
+    sib_w1 = send(w1_ref, wc.at[:, HID : 2 * HID], sibling)
+    sib_w2 = send(w2_ref, wt.at[0, HID : 2 * HID], sibling)
+    gb_z = []
+    for js, d in ((slice(4, 8), -2), (slice(0, 4), 2)):
+        arrived([gb_y[j] for j in range(js.start, js.stop) if j != home])
+        for to in (d, 1, -1):
+            gb_z.append(send(xbk.at[js, 0], xbk.at[js, -to % NL], on_z(to)))
     ga_far = []
     for way, ks in ((1, slice(0, 2)), (-1, slice(2, 4))):
         arrived([ga_y[2 * way]])
@@ -256,6 +261,10 @@
         ag[mine] = fold(value).reshape(32, 3 * HID).astype(bf16)
         x_out[h] = [send(ag.at[mine], ag.at[mine], on_x(d)) for d in (2, 1, 3)]
 
+    arrived(xs)
+    for g in range(4):
+        tails(xst, xsa, xsb, g)
+
     def outputs(h):
         js = slice(4 * h, 4 * h + 4)
         u = unfold(ag[js].astype(f32).reshape(16, 8, 3 * HID)).reshape(128, 4 * HID)
@@ -267,35 +276,20 @@
         fwd = fold(fwd.reshape(16, 8, FEAT))
         bwd = fold(bwd.reshape(16, 8, FEAT))
         value = jnp.concatenate([fwd, bwd], axis=1).astype(bf16)
-        ysa[js] = value[:, :, 0:WA].reshape(4, NL, BLOCK, WA)
-        ysb[js] = value[:, :, WA:].reshape(4, NL, BLOCK, WB)
-
-    ra_y, rb_z, relay = [], [], []
+        ysa[js] = value[:, :, 0:RA].reshape(4, NL, BLOCK, RA)
+        ysb[js] = value[:, :, RA:].reshape(4, NL, BLOCK, RB)
+
+    ra_y, rb_z = [], ([], [])
     for h in range(2):
         arrived(x_out[h])
         outputs(h)
         js = slice(4 * h, 4 * h + 4)
+        for j in range(4 * h, min(4 * h + 4, NY - 1)):
+            ra_y.append(send(ysa.at[j], ray.at[j], on_y(FAR[j])))
         d = (2, -2)[h]
-        rb_z.append(send(ysb.at[js, 2], rbz.at[2, js], on_z(d)))
+        rb_z[h].append(send(ysb.at[js, 2], rbz.at[2, js], on_z(d)))
         for w, d in enumerate((1, -1)):
-            rb_z.append(send(ysb.at[js, d % NL], rbz.at[w, js], on_z(d)))
-        for way, ks in ((1, slice(0, 2)), (-1, slice(2, 4))):
-            w = (1 - way) // 2
-            if h == 0:
-                relay.append(send(ysa.at[place(3 * way)], rel.at[w], on_y(way)))
-                far = send(ysa.at[place(4), ks], rel.at[2 + w, ks], on_y(2 * way))
-                relay.append(far)
-            else:
-                ra_y.append(send(ysa.at[place(way)], ray.at[w], on_y(way)))
-
-    arrived(relay)
-    for way, ks in ((1, slice(0, 2)), (-1, slice(2, 4))):
-        w = (1 - way) // 2
-        value = ysa[place(2 * way)].astype(f32) + rel[w].astype(f32)
-        extra = rel[2 + w, ks].astype(f32)
-        rel2[w] = value.astype(bf16)
-        rel2[w, ks] = (value[ks] + extra).astype(bf16)
-        ra_y.append(send(rel2.at[w], ray.at[2 + w], on_y(2 * way)))
+            rb_z[h].append(send(ysb.at[js, d % NL], rbz.at[w, js], on_z(d)))
 
     ag_sib = send(ag, ags, sibling)
 
@@ -307,12 +301,21 @@
         both = jnp.concatenate([first, second], axis=1)
         return both.reshape(512, 2 * HID).astype(bf16)
 
+    def part_b_y(h):
+        arrived(rb_z[h])
+        js = slice(4 * h, 4 * h + 4)
+        value = ysb[js, 0].astype(f32)
+        for w in range(3):
+            value = value + rbz[w, js].astype(f32)
+        sby[js] = value.astype(bf16)
+        return [
+            send(sby.at[j], rby.at[j], on_y(FAR[j]))
+            for j in range(4 * h, min(4 * h + 4, NY - 1))
+        ]
+
+    rb_y = part_b_y(0)
+    rb_y += part_b_y(1)
     mt[:, 0:512] = spread(ag[...], slice(0, 2 * HID)).T
-    arrived(xs)
-    for g in range(4):
-        tails(xst, xsa, xsb, g)
-    arrived([ag_sib])
-    mt[:, 512:1024] = spread(ags[...], slice(2 * HID, 4 * HID)).T
 
     def weight_grads(src, src_sib, width, first):
         for n in range(0, width, 256):
@@ -326,23 +329,17 @@
             g1v[cols, :] = g[0:HID].T
             g2v[:, cols] = g[HID:]
 
-    weight_grads(xa, xsa, WA, 0)
-
-    arrived(rb_z)
-    value = ysb[:, 0].astype(f32)
-    for w in range(3):
-        value = value + rbz[w].astype(f32)
-    sby[...] = value.astype(bf16)
-    rb_y = [send(sby.at[j], rby.at[j], on_y(FAR[j])) for j in range(NY - 1)]
-    weight_grads(xbk, xsb, WB, WA)
+
+    arrived([ag_sib])
+    mt[:, 512:1024] = spread(ags[...], slice(2 * HID, 4 * HID)).T
 
     arrived(ra_y)
     value = ysa[home].astype(f32)
-    for j in range(4):
+    for j in range(NY - 1):
         value = value + ray[j].astype(f32)
     saz[...] = value.astype(bf16)
     ra_z = [send(saz.at[d % NL], rza.at[w], on_z(d)) for w, d in enumerate((1, -1))]
-    for d, cols in ((2, slice(0, WC)), (-2, slice(WC, WA))):
+    for d, cols in ((2, slice(0, RC)), (-2, slice(RC, RA))):
         ra_z.append(send(saz.at[2, :, cols], rza.at[2, :, cols], on_z(d)))
     weight_grads(xt, xst, TAIL, FOLD)
 
@@ -358,6 +355,8 @@
         value = value + rza[w].astype(f32)
     vha[f] = value.astype(bf16)
     last += [send(vha.at[f], vha.at[f], on_z(d)) for d in (4, -4)]
+    weight_grads(xa, xsa, WA, 0)
+    weight_grads(xbk, xsb, WB, WA)
     arrived(last)
     value = jnp.concatenate(
         [
@@ -424,18 +423,16 @@
             buf(2, 3, 32, 3 * HID),
             buf(NY, 32, 3 * HID),
             buf(NY, 32, 3 * HID),
-            buf(NY, NL, BLOCK, WA),
-            buf(NY, NL, BLOCK, WB),
-            buf(4, NL, BLOCK, WA),
-            buf(2, NL, BLOCK, WA),
-            buf(4, NL, BLOCK, WA),
-            buf(3, BLOCK, WA),
-            buf(NL, BLOCK, WA),
-            buf(3, NY, BLOCK, WB),
-            buf(NY, BLOCK, WB),
-            buf(NY - 1, BLOCK, WB),
-            buf(NH, BLOCK, WA),
-            buf(NH, BLOCK, WB),
+            buf(NY, NL, BLOCK, RA),
+            buf(NY, NL, BLOCK, RB),
+            buf(NY - 1, NL, BLOCK, RA),
+            buf(3, BLOCK, RA),
+            buf(NL, BLOCK, RA),
+            buf(3, NY, BLOCK, RB),
+            buf(NY, BLOCK, RB),
+            buf(NY - 1, BLOCK, RB),
+            buf(NH, BLOCK, RA),
+            buf(NH, BLOCK, RB),
             buf(2 * HID, 1024),
             pltpu.SemaphoreType.DMA((N_SEMS,)),
             pltpu.SemaphoreType.DMA((N_SEMS,)),

time: 64.6 us -> 62.2 us (0.963)
  Pallas kernels: 63.8 us -> 61.5 us
    pallas_call x1, Pallas kernels: 62.6 us -> 60.3 us  [per_device(): pl.pallas_call(kernel, out_shape=tuple((pltpu.VMEM(*shape) for shape in s...]
where the time goes in v4:
time: 62.2 us; the launch traced here: 62.1 us
  Pallas kernels  61.5 us (99%)
  between operations  0.64 us (1%)
    pallas_call x1, Pallas kernels, per_device(): pl.pallas_call(kernel, out_shape=tuple((pltpu.VMEM(*shape) for shape in s...  60.3 us

profile of v4, /device:TPU:8, one launch (start us, length us, event | category | flops | bytes accessed | tf_op | source)
XLA Modules:
  0.0 62.1 jit_solution(3020557522924755332)
XLA Ops:
  0.6 60.3 %shard_map.84 = (bf16[6,1536]{1,0:T(8,128)(2,1)S(1)}, bf16[6,1536]{1,0:T(8,128)(2,1)S(1)}, f32[1536,128]{1,0:T(8,128)S(1)}, f32[128,1536]{1,0:T(8,128)S(1)}) custom-call(bf16[6,1536]{1,0:T(8,128)(2,1)} %tok_hbm.1, bf16[6,1536]{1,0:T(8,128)(2,1)} %cot_hbm.1, s32[16]{0:T(128)} %len_hbm.1, bf16[1536,128]{1,0:T(8,128)(2,1)} %w1_ref.1, bf16[128,1536]{1,0:T(8,128)(2,1)} %w2_ref.1), custom_call_target="tpu_custom_call" | custom-call | tf_op jit(solution)/shard_map/pallas_call | solution.py:402
  60.9 1.2 %shard_map.85 = (bf16[6,1536]{1,0:T(8,128)(2,1)}, bf16[6,1536]{1,0:T(8,128)(2,1)}, f32[1536,128]{1,0:T(8,128)}, f32[128,1536]{1,0:T(8,128)}) custom-call(bf16[6,1536]{1,0:T(8,128)(2,1)S(1)} %get-tuple-element.8.refs_0_, bf16[6,1536]{1,0:T(8,128)(2,1)S(1)} %get-tuple-element.9.refs_1_, f32[1536,128]{1,0:T(8,128)S(1)} %get-tuple-element.10.refs_2_, ...), custom_call_target="tpu_custom_call" | custom-call | tf_op jit(solution)/shard_map/pallas_call | solution.py:445

commit v5 on v4

--- a/solution.py
+++ b/solution.py
@@ -240,7 +240,6 @@
         for d in (2, 1, 3):
             j = 4 * h + lax.rem(x + d, NX)
             x_in[h].append(send(rs.at[j], rr.at[h, d - 1], on_x(d)))
-    xs = [send(xa, xsa, sibling), send(xbk, xsb, sibling)]
     x_out = {}
     for h in range(2):
         arrived(x_in[h])
@@ -261,9 +260,7 @@
         ag[mine] = fold(value).reshape(32, 3 * HID).astype(bf16)
         x_out[h] = [send(ag.at[mine], ag.at[mine], on_x(d)) for d in (2, 1, 3)]
 
-    arrived(xs)
-    for g in range(4):
-        tails(xst, xsa, xsb, g)
+    xs = [send(xa, xsa, sibling), send(xbk, xsb, sibling)]
 
     def outputs(h):
         js = slice(4 * h, 4 * h + 4)
@@ -330,6 +327,9 @@
             g2v[:, cols] = g[HID:]
 
 
+    arrived(xs)
+    for g in range(4):
+        tails(xst, xsa, xsb, g)
     arrived([ag_sib])
     mt[:, 512:1024] = spread(ags[...], slice(2 * HID, 4 * HID)).T
 
@@ -343,18 +343,18 @@
         ra_z.append(send(saz.at[2, :, cols], rza.at[2, :, cols], on_z(d)))
     weight_grads(xt, xst, TAIL, FOLD)
 
+    arrived(ra_z)
+    value = saz[0].astype(f32)
+    for w in range(3):
+        value = value + rza[w].astype(f32)
+    vha[f] = value.astype(bf16)
+    last = [send(vha.at[f], vha.at[f], on_z(d)) for d in (4, -4)]
     arrived(rb_y)
     value = sby[home].astype(f32)
     for j in range(NY - 1):
         value = value + rby[j].astype(f32)
     vhb[f] = value.astype(bf16)
-    last = [send(vhb.at[f], vhb.at[f], on_z(d)) for d in (4, -4)]
-    arrived(ra_z)
-    value = saz[0].astype(f32)
-    for w in range(3):
-        value = value + rza[w].astype(f32)
-    vha[f] = value.astype(bf16)
-    last += [send(vha.at[f], vha.at[f], on_z(d)) for d in (4, -4)]
+    last += [send(vhb.at[f], vhb.at[f], on_z(d)) for d in (4, -4)]
     weight_grads(xa, xsa, WA, 0)
     weight_grads(xbk, xsb, WB, WA)
     arrived(last)

time: 62.2 us -> 61.7 us (level)
  the two profiles are of different devices: /device:TPU:8 before, /device:TPU:4 now
where the time goes in v5:
time: 61.7 us; the launch traced here: 61.6 us
  Pallas kernels  60.9 us (99%)
  between operations  0.64 us (1%)
    pallas_call x1, Pallas kernels, per_device(): pl.pallas_call(kernel, out_shape=tuple((pltpu.VMEM(*shape) for shape in s...  59.8 us

profile of v5, /device:TPU:4, one launch (start us, length us, event | category | flops | bytes accessed | tf_op | source)
XLA Modules:
  0.0 61.6 jit_solution(12598659170578337721)
XLA Ops:
  0.6 59.8 %shard_map.84 = (bf16[6,1536]{1,0:T(8,128)(2,1)S(1)}, bf16[6,1536]{1,0:T(8,128)(2,1)S(1)}, f32[1536,128]{1,0:T(8,128)S(1)}, f32[128,1536]{1,0:T(8,128)S(1)}) custom-call(bf16[6,1536]{1,0:T(8,128)(2,1)} %tok_hbm.1, bf16[6,1536]{1,0:T(8,128)(2,1)} %cot_hbm.1, s32[16]{0:T(128)} %len_hbm.1, bf16[1536,128]{1,0:T(8,128)(2,1)} %w1_ref.1, bf16[128,1536]{1,0:T(8,128)(2,1)} %w2_ref.1), custom_call_target="tpu_custom_call" | custom-call | tf_op jit(solution)/shard_map/pallas_call | solution.py:402
  60.4 1.2 %shard_map.85 = (bf16[6,1536]{1,0:T(8,128)(2,1)}, bf16[6,1536]{1,0:T(8,128)(2,1)}, f32[1536,128]{1,0:T(8,128)}, f32[128,1536]{1,0:T(8,128)}) custom-call(bf16[6,1536]{1,0:T(8,128)(2,1)S(1)} %get-tuple-element.8.refs_0_, bf16[6,1536]{1,0:T(8,128)(2,1)S(1)} %get-tuple-element.9.refs_1_, f32[1536,128]{1,0:T(8,128)S(1)} %get-tuple-element.10.refs_2_, ...), custom_call_target="tpu_custom_call" | custom-call | tf_op jit(solution)/shard_map/pallas_call | solution.py:445
